TPU v7x, 32 devices: a whole 2x2x4 slice. The times are simulated.
32 devices in a mesh: row: 4 (over y, x), col: 2 (over core), layer: 4 (over z).
Axes of the slice: x: 2, y: 2, z: 4, core: 2. Of those that a mesh axis runs over, the one named last changes fastest.
Arguments:
- a_blocks: bfloat16 [4, 2, 16, 64, 512], P('layer', None, ('row', 'col')), may hold values from -0.09375 to 0.09375
- a_cols: int32 [4, 2, 16, 8], P('layer', None, ('row', 'col')), may hold values from 0 to 7
- p_blocks: bfloat16 [4, 2, 2, 8, 64, 256], P('layer', None, 'col', 'row'), may hold values from -12 to 12
- p_cols: int32 [4, 2, 2, 8, 4], P('layer', None, 'col', 'row'), may hold values from 0 to 15, as said below
- c_cols: int32 [2, 16, 8], P('col', 'row'), may hold values from 0 to 15, as said below
Outputs:
- c_blocks: bfloat16 [2, 16, 64, 512], P('col', ('row', 'layer'))
Inputs may be any that keep to these rules, and one draw needn't show every extreme that they name: `p_cols`: the 4 entries of a block row of P in one column group are distinct. `c_cols`: the 8 entries of a block row of C in one column group are distinct.
All inputs are finite; a program needn't handle non-finite values.
Results may differ from a plain program's by a relative error of at most 0.008.
Values may be sent and summed in bfloat16 or wider, within the bound.
A program may use at most 64 MiB of HBM per device.

v0:
```python
import jax
import jax.numpy as jnp
from jax import lax
from jax.sharding import PartitionSpec as P

SECTIONS = 2


def block_terms(a_strip, row_idx, p_panel, panel_idx, targets):
    row_count = a_strip.shape[0]
    side = a_strip.shape[1]
    couple = row_idx.shape[1]
    fine_slots = panel_idx.shape[1]
    coarse_slots = targets.shape[1]
    picked = p_panel[row_idx]
    a_four = a_strip.reshape(row_count, side, couple, side)
    prods = jnp.einsum("ixky,ikyz->ikxz", a_four, picked, preferred_element_type=jnp.float32)
    prods = prods.reshape(row_count, couple, side, fine_slots, side)
    coarse = panel_idx[row_idx]
    onehot = (coarse[:, :, :, None] == targets[:, None, None, :]).astype(jnp.float32)
    placed = jnp.einsum("ikxjz,ikjm->ixmz", prods, onehot, preferred_element_type=jnp.float32)
    return placed.reshape(row_count, side, coarse_slots * side)


def local(a_blocks, a_cols, p_blocks, p_cols, c_cols):
    targets = c_cols[0]
    group_rows = targets.shape[0]
    side = a_blocks.shape[3]
    strips, indices = (
        lax.all_gather(a_blocks[0], "col", axis=1, tiled=True),
        lax.all_gather(a_cols[0], "col", axis=1, tiled=True),
    )
    panels, panel_cols = (
        lax.all_gather(p_blocks[0, :, 0], "row", axis=1, tiled=True),
        lax.all_gather(p_cols[0, :, 0], "row", axis=1, tiled=True),
    )
    gathered = [
        (strips[section_no], indices[section_no], panels[section_no], panel_cols[section_no])
        for section_no in range(SECTIONS)
    ]
    own_rows = group_rows // lax.axis_size("layer")
    running = jnp.zeros(
        (lax.axis_size("layer") * own_rows, side, targets.shape[1] * side), jnp.float32
    )
    for a_strip, row_idx, p_panel, panel_idx in gathered:
        running = running + block_terms(a_strip, row_idx, p_panel, panel_idx, targets)
    shares = lax.psum_scatter(running, "layer", scatter_dimension=0, tiled=True)
    return shares.astype(jnp.bfloat16)[None]


def solution(mesh):
    return jax.shard_map(
        local,
        mesh=mesh,
        in_specs=(
            P("layer", None, ("row", "col"), None, None),
            P("layer", None, ("row", "col"), None),
            P("layer", None, "col", "row", None, None),
            P("layer", None, "col", "row", None),
            P("col", "row", None),
        ),
        out_specs=P("col", ("row", "layer"), None, None),
        check_vma=False,
    )
```

profile of v0, /device:TPU:0, one launch (start us, length us, event | category | flops | bytes accessed | tf_op | source)
XLA Modules:
  0.0 77.6 jit_solution(16574627112151271226)
XLA Ops:
  6.5 0.0 reduce-scatter.2.cloned.1.call-start
  6.5 0.7 copy.30
  7.2 1.9 %all-gather.1 = s32[1,2,4,8]{3,1,0,2:T(2,128)S(1)} all-gather(s32[1,2,2,8]{3,1,0,2:T(2,128)S(1)} %copy.30), channel_id=3, replica_groups=mesh['row'=4,'col'=2,'layer'=4] {'col'}, dimensions={2}, use_global_device_ids=true | all-gather | bytes 384 | tf_op jit(solution)/shard_map/all_gather | solution.py:31
  9.1 0.1 reshape.72
  9.2 0.0 copy-start.2
  9.2 12.5 %all-gather.2 = bf16[1,2,1,8,64,256]{5,4,3,2,1,0:T(8,128)(2,1)S(1)} all-gather(bf16[1,2,1,2,64,256]{5,4,3,2,1,0:T(8,128)(2,1)} %param.7), channel_id=4, replica_groups=mesh['row'=4,'col'=2,'layer'=4] {'row'}, dimensions={3}, use_global_device_ids=true | all-gather | bytes 655360 | tf_op jit(solution)/shard_map/all_gather | solution.py:34
  21.8 2.4 %all-gather.3 = bf16[1,2,4,64,512]{4,3,2,1,0:T(8,128)(2,1)S(1)} all-gather(bf16[1,2,2,64,512]{4,3,2,1,0:T(8,128)(2,1)} %param.5), channel_id=5, replica_groups=mesh['row'=4,'col'=2,'layer'=4] {'col'}, dimensions={2}, use_global_device_ids=true | all-gather | bytes 786432 | tf_op jit(solution)/shard_map/all_gather | solution.py:30
  24.1 0.7 fusion.26
  24.9 0.3 reshape_squeeze.6
  25.2 0.0 copy-done.2
  25.2 0.6 gather_fusion.1
  25.8 0.4 convolution_bitcast_fusion.1
  26.2 0.9 %reshape.68 = bf16[4,8,64,4,64]{4,3,2,1,0:T(4,128)(2,1)S(1)} reshape(bf16[4,8,64,256]{3,2,1,0:T(8,128)(2,1)S(1)} %convolution_bitcast_fusion.1) | data formatting | bytes 2097152 | tf_op jit(solution)/shard_map/reshape | solution.py:18
  27.1 7.1 %all-gather = s32[1,2,1,8,4]{4,1,2,0,3:T(2,128)S(1)} all-gather(s32[1,2,1,2,4]{4,1,2,0,3:T(2,128)S(1)} %copy.28), channel_id=2, replica_groups=mesh['row'=4,'col'=2,'layer'=4] {'row'}, dimensions={3}, use_global_device_ids=true | all-gather | bytes 320 | tf_op jit(solution)/shard_map/all_gather | solution.py:35
  34.2 0.6 gather_fusion
  34.8 0.1 copy.33
  34.9 0.1 reshape.88
  35.0 2.1 %reshape_squeeze.7 = bf16[4,64,8,64]{3,2,1,0:T(8,128)(2,1)} reshape(bf16[1,1,4,64,512]{4,3,2,1,0:T(8,128)(2,1)} %get-tuple-element.5) | data formatting | bytes 524288 | tf_op jit(solution)/shard_map/reshape;squeeze | solution.py:16
  37.0 1.6 %gather_fusion.3 = bf16[32,64,256]{2,1,0:T(8,128)(2,1)} fusion(bf16[8,64,256]{2,1,0:T(8,128)(2,1)S(1)} %get-tuple-element.7, s32[1024]{0:T(1024)S(1)} %pad_clamp_fusion), kind=kCustom, calls=%fused_computation.3 | custom fusion | bytes 2097280 | tf_op jit(solution)/shard_map/gather | solution.py:15
  38.6 1.8 %convolution_bitcast_fusion = bf16[4,8,64,256]{3,2,1,0:T(8,128)(2,1)S(1)} fusion(bf16[4,8,64,256]{3,2,1,0:T(8,128)(2,1)} %bitcast.60, bf16[4,64,8,64]{3,2,1,0:T(8,128)(2,1)} %reshape_squeeze.7), kind=kOutput, calls=%fused_computation.8 | convolution fusion | flops 67108864 | bytes 2359296 | tf_op jit(solution)/shard_map/ixky,ikyz->ikxz/dot_general | solution.py:17
  40.4 0.0 copy-start.1
  40.4 1.9 %reshape.69 = bf16[4,8,64,4,64]{4,3,2,1,0:T(4,128)(2,1)} reshape(bf16[4,8,64,256]{3,2,1,0:T(8,128)(2,1)S(1)} %convolution_bitcast_fusion) | data formatting | bytes 2097152 | tf_op jit(solution)/shard_map/reshape | solution.py:18
  42.3 0.6 gather_fusion.2
  42.9 0.1 copy.39
  43.0 0.0 copy-start
  43.0 0.0 copy-done.1
  43.0 1.4 %fusion.4 = f32[4,8,64,64]{3,1,2,0:T(8,128)S(1)} fusion(bf16[4,8,64,4,64]{4,3,2,1,0:T(4,128)(2,1)S(1)} %reshape.68, s32[4,8]{1,0:T(4,128)S(1)} %bitcast.65, s32[4,8,4]{1,2,0:T(4,128)S(1)} %copy.33), kind=kOutput, calls=%fused_computation.10 | convolution fusion | flops 8389632 | bytes 1573504 | tf_op jit(solution)/shard_map/ikxjz,ikjm->ixmz/dot_general | solution.py:21
  44.4 0.2 copy-done
  44.6 1.4 %fusion.13 = f32[4,64,8,64]{3,2,1,0:T(8,128)S(1)} fusion(f32[4,8,64,64]{3,1,2,0:T(8,128)S(1)} %fusion.4, bf16[4,8,64,4,64]{4,3,2,1,0:T(4,128)(2,1)S(1)} %copy-done, s32[4,8,4]{1,2,0:T(4,128)S(1)} %copy.39, s32[4,8]{1,0:T(4,128)S(1)} %bitcast.66), kind=kOutput, calls=%fused_computation.13 | convolution fusion | flops 8520704 | bytes 2097792 | tf_op jit(solution)/shard_map/ikxjz,ikjm->ixmz/dot_general | solution.py:21
  46.0 1.1 %add.37 = f32[4,64,512]{2,1,0:T(8,128)} reshape(f32[4,64,8,64]{3,2,1,0:T(8,128)S(1)} %fusion.13) | data formatting | bytes 1048576 | tf_op jit(solution)/shard_map/add | solution.py:46
  47.1 0.0 reduce-scatter.2.cloned.1.call-update
  47.1 22.1 %reduce-scatter.2.cloned.1.call-done = f32[1,64,512]{2,1,0:T(8,128)} async-done(((f32[4,64,512]{2,1,0:T(8,128)}), f32[1,64,512]{2,1,0:T(8,128)}) %reduce-scatter.2.cloned.1.call-update) | async-done | bytes 131088 | tf_op jit(solution)/shard_map/reduce_scatter | solution.py:47
  69.2 1.5 %convert_bitcast_fusion = bf16[1,1,64,512]{3,2,1,0:T(8,128)(2,1)} fusion(f32[1,64,512]{2,1,0:T(8,128)} %reduce-scatter.2.cloned.1.call-done), kind=kLoop, calls=%fused_computation.18 | loop fusion | flops 32768 | bytes 196608 | tf_op jit(solution)/shard_map/broadcast_in_dim | solution.py:48
  (8 shorter events, 0.1 us)
Async XLA Ops:
  6.5 62.6 %reduce-scatter.2.cloned.1.call-start = ((), (), s32[]{:S(2)}) async-start(), calls=%async_computation.1 | async-start | bytes 655360 | tf_op jit(solution)/shard_map/reduce_scatter | solution.py:47
  9.2 15.9 %copy-start.2 = (s32[1,2,1,2,4]{4,3,2,1,0:T(2,128)S(1)}, s32[1,2,1,2,4]{4,3,2,1,0:T(2,128)}, u32[]{:S(2)}) copy-start(s32[1,2,1,2,4]{4,3,2,1,0:T(2,128)} %param.8) | copy-start | bytes 196
  40.4 2.6 %copy-start.1 = (s32[1,4,8]{2,1,0:T(4,128)S(1)}, s32[1,4,8]{2,1,0:T(4,128)}, u32[]{:S(2)}) copy-start(s32[1,4,8]{2,1,0:T(4,128)} %param.9) | copy-start | bytes 388
  43.0 1.6 %copy-start = (bf16[4,8,64,4,64]{4,3,2,1,0:T(4,128)(2,1)S(1)}, bf16[4,8,64,4,64]{4,3,2,1,0:T(4,128)(2,1)}, u32[]{:S(2)}) copy-start(bf16[4,8,64,4,64]{4,3,2,1,0:T(4,128)(2,1)} %reshape.69) | copy-start | bytes 3145732
Sparse Core Ops, SparseCore 0:
  47.2 21.9 reduce-scatter.1
where the time goes:
time: 77.9 us; the launch traced here: 77.6 us
  blocking collectives  23.9 us (31%)
  waiting for transfers between devices  22.1 us (28%)
  between operations  13.5 us (17%)
  local copies, waits for them, and re-layouts  11.5 us (15%)
  matrix products  5.03 us (6%)
  other arithmetic  1.57 us (2%)
    reduce_scatter x1, waiting for transfers between devices, local(): shares = lax.psum_scatter(running, 'layer', scatter_dimension=0, tiled=True)  22.1 us
    all_gather x1, blocking collectives, local(): lax.all_gather(p_blocks[0, :, 0], 'row', axis=1, tiled=True)  12.5 us
    all_gather x1, blocking collectives, local(): lax.all_gather(p_cols[0, :, 0], 'row', axis=1, tiled=True)  7.08 us
    dot_general x2, matrix products, block_terms(): jnp.einsum('ikxjz,ikjm->ixmz', prods, onehot, preferred_element_type=jnp....  2.83 us
    reshape x2, local copies, waits for them, and re-layouts, block_terms(): prods = prods.reshape(row_count, couple, side, fine_slots, side)  2.75 us
    all_gather x1, blocking collectives, local(): lax.all_gather(a_blocks[0], 'col', axis=1, tiled=True)  2.39 us
    another operation x2, local copies, waits for them, and re-layouts, block_terms(): a_four = a_strip.reshape(row_count, side, couple, side)  2.35 us
    dot_general x2, matrix products, block_terms(): jnp.einsum('ixky,ikyz->ikxz', a_four, picked, preferred_element_type=jnp....  2.2 us
  transfers between devices with their start and end apart: 1, of which 1 were waited for; matrix products, arithmetic and copies ran while one was open for 0% of the time, Pallas kernels for 0%

commit v1 on v0

v1 whole, which is shorter than its diff:
```python
import functools

import jax
import jax.numpy as jnp
from jax import lax
from jax.experimental import pallas as pl
from jax.experimental.pallas import tpu as pltpu
from jax.sharding import PartitionSpec as P

MESH = pl.DeviceIdType.MESH
LANES = 128
NCC = 16


def partner(me, d, n):
    out = 0
    bit = 1
    while bit < n:
        out = out + lax.rem(lax.div(me, bit) + ((d // bit) % 2), 2) * bit
        bit *= 2
    return out


def pair_codes(values, half):
    lane = lax.broadcasted_iota(jnp.int32, (1, LANES), 1)
    low = lane < half
    codes = []
    for p in range(len(values) // 2):
        codes.append(jnp.where(low, values[2 * p], values[2 * p + 1]))
        codes.append(jnp.where(low, values[2 * p + 1], values[2 * p]))
    return codes


def pair_tiles(x, half):
    tiles = []
    for p in range(x.shape[1] // LANES):
        tile = x[:, p * LANES:(p + 1) * LANES].astype(jnp.float32)
        tiles.append(tile)
        tiles.append(pltpu.roll(tile, half, axis=1))
    return tiles


def kernel(dims, a_hbm, a_cols, p_hbm, p_cols, c_cols, out_ref,
           a_v, p_all, code_all, at_all, spread, t_acc, t_pick, own, c_send, c_recv,
           in_sem, ps, pr, cs, cr, as_, ar, zs, zr):
    n_row, n_col, n_layer = dims
    sections, rl, side, width = a_v.shape
    rp = p_all.shape[2]
    group = at_all.shape[0] * rl
    own_rows = c_send.shape[1]
    kc = c_cols.shape[2]
    my_row, my_col, my_layer = (lax.axis_index(x) for x in ("row", "col", "layer"))

    barrier = pltpu.get_barrier_semaphore()
    for axis, me, n in (("row", my_row, n_row), ("col", my_col, n_col), ("layer", my_layer, n_layer)):
        for d in range(1, n):
            pl.semaphore_signal(barrier, inc=1, device_id={axis: partner(me, d, n)}, device_id_type=MESH)

    load_p = pltpu.make_async_copy(p_hbm.at[0, :, 0], p_all.at[my_row], in_sem.at[0])
    load_a = pltpu.make_async_copy(a_hbm.at[0], a_v, in_sem.at[1])
    load_p.start()
    load_a.start()

    lane = lax.broadcasted_iota(jnp.int32, (side, LANES), 1)
    low = lane < side
    second = jnp.where(low, 0, 1)

    per_row = p_cols.shape[4]
    for s in range(sections):
        for r in range(rp):
            codes = pair_codes([p_cols[0, s, 0, r, j] for j in range(per_row)], side)
            for v, code in enumerate(codes):
                at = (s * rp + r) * per_row + v
                code_all[my_row, at:at + 1, :] = code

    load_a.wait()
    for s in range(sections):
        for i in range(rl):
            codes = pair_codes([a_cols[0, s, i, k] for k in range(width // side)], side)
            codes = [jnp.broadcast_to(code, (side, LANES)) for code in codes]
            tiles = pair_tiles(a_v[s, i], side)
            for q in range(n_row * rp // 2):
                total = jnp.zeros((side, LANES), jnp.float32)
                for code, tile in zip(codes, tiles):
                    total = total + jnp.where(code == 2 * q + second, tile, 0.0)
                slot = 2 * q // rp
                start = (s * rp + 2 * q % rp) * side
                at_all[my_col, slot, i * side:(i + 1) * side, start:start + LANES] = total.astype(jnp.bfloat16)

    load_p.wait()
    pl.semaphore_wait(barrier, (n_row - 1) + (n_col - 1) + (n_layer - 1))

    sends = []
    p_copies, a_copies = [], []
    for d in range(1, n_row):
        to = {"row": partner(my_row, d, n_row)}
        code_copy = pltpu.make_async_remote_copy(
            code_all.at[my_row], code_all.at[my_row], cs.at[d - 1], cr.at[d - 1], device_id=to, device_id_type=MESH)
        code_copy.start()
        copy = pltpu.make_async_remote_copy(
            p_all.at[my_row], p_all.at[my_row], ps.at[d - 1], pr.at[d - 1], device_id=to, device_id_type=MESH)
        copy.start()
        p_copies.append((code_copy, copy))
        sends += [code_copy, copy]
    for d in range(1, n_col):
        copy = pltpu.make_async_remote_copy(
            at_all.at[my_col], at_all.at[my_col], as_.at[d - 1], ar.at[d - 1],
            device_id={"col": partner(my_col, d, n_col)}, device_id_type=MESH)
        copy.start()
        a_copies.append(copy)
        sends.append(copy)

    def spread_rows(slot, to):
        for s in range(sections):
            for r in range(rp):
                codes = []
                for v in range(per_row):
                    at = (s * rp + r) * per_row + v
                    codes.append(jnp.broadcast_to(code_all[slot, at:at + 1, :], (side, LANES)))
                tiles = pair_tiles(p_all[slot, s, r], side)
                for q in range(NCC // 2):
                    total = jnp.zeros((side, LANES), jnp.float32)
                    for code, tile in zip(codes, tiles):
                        total = jnp.where(code == 2 * q + second, tile, total)
                    first = (s * rp + r) * side
                    spread[to, first:first + side, q * LANES:(q + 1) * LANES] = total.astype(jnp.bfloat16)

    step_cols = 2 * LANES
    for d in range(n_row):
        slot = partner(my_row, d, n_row)
        if d > 0:
            for copy in p_copies[d - 1]:
                copy.wait_recv()
        spread_rows(slot, d)
        if d == 0:
            for copy in a_copies:
                copy.wait_recv()
        left = at_all[:, slot].reshape(group * side, sections * rp * side)
        for n in range(0, NCC * side, step_cols):
            part = jnp.dot(left, spread[d, :, n:n + step_cols], preferred_element_type=jnp.float32)
            if d > 0:
                part = part + t_acc[:, n:n + step_cols]
            if d < n_row - 1:
                t_acc[:, n:n + step_cols] = part
            else:
                for i in range(group):
                    for h in range(step_cols // LANES):
                        tile = part[i * side:(i + 1) * side, h * LANES:(h + 1) * LANES]
                        q = n // LANES + h
                        t_pick[i, q] = tile
                        t_pick[i, NCC // 2 + q] = pltpu.roll(tile, side, axis=1)

    def pick(i, u):
        c0 = c_cols[0, i, 2 * u]
        c1 = c_cols[0, i, 2 * u + 1]
        at0 = lax.rem(c0, 2) * (NCC // 2) + lax.div(c0, 2)
        at1 = (1 - lax.rem(c1, 2)) * (NCC // 2) + lax.div(c1, 2)
        return jnp.where(low, t_pick[i, at0], t_pick[i, at1])

    z_copies = []
    for d in range(n_layer - 1, 0, -1):
        dst = partner(my_layer, d, n_layer)
        for o in range(own_rows):
            for u in range(kc // 2):
                c_send[d - 1, o, :, u * LANES:(u + 1) * LANES] = pick(dst * own_rows + o, u).astype(jnp.bfloat16)
        copy = pltpu.make_async_remote_copy(
            c_send.at[d - 1], c_recv.at[d - 1], zs.at[d - 1], zr.at[d - 1],
            device_id={"layer": dst}, device_id_type=MESH)
        copy.start()
        z_copies.append(copy)
        sends.append(copy)
    for o in range(own_rows):
        for u in range(kc // 2):
            own[o, :, u * LANES:(u + 1) * LANES] = pick(my_layer * own_rows + o, u)
    for copy in reversed(z_copies):
        copy.wait_recv()
    total = own[...]
    for d in range(1, n_layer):
        total = total + c_recv[d - 1].astype(jnp.float32)
    out_ref[0] = total.astype(jnp.bfloat16)
    for copy in sends:
        copy.wait_send()


def local(dims, a_blocks, a_cols, p_blocks, p_cols, c_cols):
    n_row, n_col, n_layer = dims
    sections, rl, side, width = a_blocks.shape[1:]
    rp, p_width = p_blocks.shape[3], p_blocks.shape[5]
    group, kc = c_cols.shape[1:]
    own_rows = group // n_layer
    codes = sections * rp * (p_width // side)
    strip = (own_rows, side, kc * side)
    depth = sections * rp * side
    dma = pltpu.SemaphoreType.DMA
    return pl.pallas_call(
        functools.partial(kernel, dims),
        out_shape=jax.ShapeDtypeStruct((1,) + strip, jnp.bfloat16),
        in_specs=[
            pl.BlockSpec(memory_space=pl.ANY),
            pl.BlockSpec(memory_space=pltpu.SMEM),
            pl.BlockSpec(memory_space=pl.ANY),
            pl.BlockSpec(memory_space=pltpu.SMEM),
            pl.BlockSpec(memory_space=pltpu.SMEM),
        ],
        out_specs=pl.BlockSpec(memory_space=pltpu.VMEM),
        scratch_shapes=[
            pltpu.VMEM((sections, rl, side, width), jnp.bfloat16),
            pltpu.VMEM((n_row, sections, rp, side, p_width), jnp.bfloat16),
            pltpu.VMEM((n_row, codes, LANES), jnp.int32),
            pltpu.VMEM((n_col, n_row, rl * side, depth), jnp.bfloat16),
            pltpu.VMEM((n_row, depth, NCC * side), jnp.bfloat16),
            pltpu.VMEM((group * side, NCC * side), jnp.float32),
            pltpu.VMEM((group, NCC, side, LANES), jnp.float32),
            pltpu.VMEM(strip, jnp.float32),
            pltpu.VMEM((n_layer - 1,) + strip, jnp.bfloat16),
            pltpu.VMEM((n_layer - 1,) + strip, jnp.bfloat16),
            dma((2,)),
            dma((n_row - 1,)), dma((n_row - 1,)),
            dma((n_row - 1,)), dma((n_row - 1,)),
            dma((n_col - 1,)), dma((n_col - 1,)),
            dma((n_layer - 1,)), dma((n_layer - 1,)),
        ],
        compiler_params=pltpu.CompilerParams(
            collective_id=0, has_side_effects=True, vmem_limit_bytes=40 * 2**20),
    )(a_blocks, a_cols, p_blocks, p_cols, c_cols)


def solution(mesh):
    dims = tuple(mesh.shape[x] for x in ("row", "col", "layer"))
    return jax.shard_map(
        functools.partial(local, dims),
        mesh=mesh,
        in_specs=(
            P("layer", None, ("row", "col"), None, None),
            P("layer", None, ("row", "col"), None),
            P("layer", None, "col", "row", None, None),
            P("layer", None, "col", "row", None),
            P("col", "row", None),
        ),
        out_specs=P("col", ("row", "layer"), None, None),
        check_vma=False,
    )
```

time: 77.9 us -> 26.4 us (0.34)
  blocking collectives: 23.9 us -> 0 us
  waiting for transfers between devices: 22.1 us -> 0 us
  Pallas kernels: 0 us -> 21.6 us
  between operations: 13.5 us -> 0.01 us
  local copies, waits for them, and re-layouts: 11.5 us -> 4.53 us
  matrix products: 5.03 us -> 0 us
  other arithmetic: 1.57 us -> 0 us
    all_gather x4 -> x0, blocking collectives: 23.9 us -> none  [the longest x1 12.5 us: local(): lax.all_gather(p_blocks[0, :, 0], 'row', axis=1, tiled=True)]
    reduce_scatter x1 -> x0, waiting for transfers between devices: 22.1 us -> none  [local(): shares = lax.psum_scatter(running, 'layer', scatter_dimension=0, tiled=True)]
    pallas_call x0 -> x1, Pallas kernels: none -> 21.6 us  [local(): pl.pallas_call(functools.partial(kernel, dims), out_shape=jax.ShapeDtypeS...]
    dot_general x4 -> x0, matrix products: 5.03 us -> none  [the longest x2 2.83 us: block_terms(): jnp.einsum('ikxjz,ikjm->ixmz', prods, onehot, preferred_element_type=jnp....]
    unnamed x8 -> x11, local copies, waits for them, and re-layouts: 0.87 us -> 4.53 us
    gather x6 -> x0, local copies, waits for them, and re-layouts: 3.54 us -> none  [the longest x2 2.19 us: block_terms(): picked = p_panel[row_idx]]
    reshape x2 -> x0, local copies, waits for them, and re-layouts: 2.75 us -> none  [block_terms(): prods = prods.reshape(row_count, couple, side, fine_slots, side)]
    another operation x2 -> x0, local copies, waits for them, and re-layouts: 2.35 us -> none  [block_terms(): a_four = a_strip.reshape(row_count, side, couple, side)]
  transfers between devices with their start and end apart: 1 -> 0, of which waited for: 1 -> 0; matrix products, arithmetic and copies ran while one was open for 0% -> 0% of each run, Pallas kernels for 0% -> 0%
where the time goes in v1:
time: 26.4 us; the launch traced here: 26.2 us
  Pallas kernels  21.6 us (82%)
  local copies, waits for them, and re-layouts  4.53 us (17%)
    pallas_call x1, Pallas kernels, local(): pl.pallas_call(functools.partial(kernel, dims), out_shape=jax.ShapeDtypeS...  21.6 us
    unnamed x11, local copies, waits for them, and re-layouts  4.53 us

profile of v1, /device:TPU:0, one launch (start us, length us, event | category | flops | bytes accessed | tf_op | source)
XLA Modules:
  0.0 26.2 jit_solution(9596436499764372892)
XLA Ops:
  0.0 0.0 copy-start
  0.0 0.9 %copy-done = bf16[1,2,2,64,512]{4,3,2,1,0:T(8,128)(2,1)S(1)} copy-done((bf16[1,2,2,64,512]{4,3,2,1,0:T(8,128)(2,1)S(1)}, bf16[1,2,2,64,512]{4,3,2,1,0:T(8,128)(2,1)}, u32[]{:S(2)}) %copy-start) | copy-done | bytes 262168
  1.0 0.0 copy-start.1
  1.0 0.9 %copy-done.1 = bf16[1,2,1,2,64,256]{5,4,3,2,1,0:T(8,128)(2,1)S(1)} copy-done((bf16[1,2,1,2,64,256]{5,4,3,2,1,0:T(8,128)(2,1)S(1)}, bf16[1,2,1,2,64,256]{5,4,3,2,1,0:T(8,128)(2,1)}, u32[]{:S(2)}) %copy-start.1) | copy-done | bytes 131096
  1.9 0.0 copy-start.2
  1.9 0.7 %copy-done.2 = s32[1,2,2,8]{3,2,1,0:T(2,128)S(1)} copy-done((s32[1,2,2,8]{3,2,1,0:T(2,128)S(1)}, s32[1,2,2,8]{3,2,1,0:T(2,128)}, u32[]{:S(2)}) %copy-start.2) | copy-done | bytes 152
  2.5 0.0 copy-start.3
  2.5 0.7 %copy-done.3 = s32[1,2,1,2,4]{4,3,2,1,0:T(2,128)S(1)} copy-done((s32[1,2,1,2,4]{4,3,2,1,0:T(2,128)S(1)}, s32[1,2,1,2,4]{4,3,2,1,0:T(2,128)}, u32[]{:S(2)}) %copy-start.3) | copy-done | bytes 88
  3.2 0.0 copy-start.4
  3.2 0.7 %copy-done.4 = s32[1,4,8]{2,1,0:T(4,128)S(1)} copy-done((s32[1,4,8]{2,1,0:T(4,128)S(1)}, s32[1,4,8]{2,1,0:T(4,128)}, u32[]{:S(2)}) %copy-start.4) | copy-done | bytes 152
  3.9 21.6 %shard_map.55 = bf16[1,1,64,512]{3,2,1,0:T(8,128)(2,1)S(1)} custom-call(bf16[1,2,2,64,512]{4,3,2,1,0:T(8,128)(2,1)S(1)} %copy-done, s32[1,2,2,8]{3,2,1,0:T(2,128)S(1)} %copy-done.2, bf16[1,2,1,2,64,256]{5,4,3,2,1,0:T(8,128)(2,1)S(1)} %copy-done.1, s32[1,2,1,2,4]{4,3,2,1,0:T(2,128)S(1)} %copy-done.3, s32[1,4,8]{2,1,0:T(4,128)S(1)} %copy-done.4), custom_call_target="tpu_custom_call" | custom-call | tf_op jit(solution)/shard_map/pallas_call | solution.py:195
  25.5 0.6 %copy.7 = bf16[1,1,64,512]{3,2,1,0:T(8,128)(2,1)} copy(bf16[1,1,64,512]{3,2,1,0:T(8,128)(2,1)S(1)} %shard_map.55) | data formatting | bytes 131072
Async XLA Ops:
  0.0 0.9 %copy-start = (bf16[1,2,2,64,512]{4,3,2,1,0:T(8,128)(2,1)S(1)}, bf16[1,2,2,64,512]{4,3,2,1,0:T(8,128)(2,1)}, u32[]{:S(2)}) copy-start(bf16[1,2,2,64,512]{4,3,2,1,0:T(8,128)(2,1)} %a_hbm.1) | copy-start | bytes 786436
  1.0 0.9 %copy-start.1 = (bf16[1,2,1,2,64,256]{5,4,3,2,1,0:T(8,128)(2,1)S(1)}, bf16[1,2,1,2,64,256]{5,4,3,2,1,0:T(8,128)(2,1)}, u32[]{:S(2)}) copy-start(bf16[1,2,1,2,64,256]{5,4,3,2,1,0:T(8,128)(2,1)} %p_hbm.1) | copy-start | bytes 393220
  1.9 0.7 %copy-start.2 = (s32[1,2,2,8]{3,2,1,0:T(2,128)S(1)}, s32[1,2,2,8]{3,2,1,0:T(2,128)}, u32[]{:S(2)}) copy-start(s32[1,2,2,8]{3,2,1,0:T(2,128)} %a_cols.1) | copy-start | bytes 388
  2.5 0.7 %copy-start.3 = (s32[1,2,1,2,4]{4,3,2,1,0:T(2,128)S(1)}, s32[1,2,1,2,4]{4,3,2,1,0:T(2,128)}, u32[]{:S(2)}) copy-start(s32[1,2,1,2,4]{4,3,2,1,0:T(2,128)} %p_cols.1) | copy-start | bytes 196
  3.2 0.7 %copy-start.4 = (s32[1,4,8]{2,1,0:T(4,128)S(1)}, s32[1,4,8]{2,1,0:T(4,128)}, u32[]{:S(2)}) copy-start(s32[1,4,8]{2,1,0:T(4,128)} %c_cols.1) | copy-start | bytes 388

commit v2 on v1

--- a/solution.py
+++ b/solution.py
@@ -40,8 +40,8 @@
     return tiles
 
 
-def kernel(dims, a_hbm, a_cols, p_hbm, p_cols, c_cols, out_ref,
-           a_v, p_all, code_all, at_all, spread, t_acc, t_pick, own, c_send, c_recv,
+def kernel(dims, a_hbm, a_cols_hbm, p_hbm, p_cols_hbm, c_cols_hbm, out_ref,
+           a_cols, p_cols, c_cols, a_v, p_all, code_all, at_all, spread, t_acc, t_pick, own, c_send, c_recv,
            in_sem, ps, pr, cs, cr, as_, ar, zs, zr):
     n_row, n_col, n_layer = dims
     sections, rl, side, width = a_v.shape
@@ -58,14 +58,18 @@
 
     load_p = pltpu.make_async_copy(p_hbm.at[0, :, 0], p_all.at[my_row], in_sem.at[0])
     load_a = pltpu.make_async_copy(a_hbm.at[0], a_v, in_sem.at[1])
-    load_p.start()
-    load_a.start()
+    load_pc = pltpu.make_async_copy(p_cols_hbm, p_cols, in_sem.at[2])
+    load_ac = pltpu.make_async_copy(a_cols_hbm, a_cols, in_sem.at[3])
+    load_cc = pltpu.make_async_copy(c_cols_hbm, c_cols, in_sem.at[4])
+    for load in (load_p, load_pc, load_ac, load_a, load_cc):
+        load.start()
 
     lane = lax.broadcasted_iota(jnp.int32, (side, LANES), 1)
     low = lane < side
     second = jnp.where(low, 0, 1)
 
     per_row = p_cols.shape[4]
+    load_pc.wait()
     for s in range(sections):
         for r in range(rp):
             codes = pair_codes([p_cols[0, s, 0, r, j] for j in range(per_row)], side)
@@ -73,6 +77,7 @@
                 at = (s * rp + r) * per_row + v
                 code_all[my_row, at:at + 1, :] = code
 
+    load_ac.wait()
     load_a.wait()
     for s in range(sections):
         for i in range(rl):
@@ -88,6 +93,7 @@
                 at_all[my_col, slot, i * side:(i + 1) * side, start:start + LANES] = total.astype(jnp.bfloat16)
 
     load_p.wait()
+    load_cc.wait()
     pl.semaphore_wait(barrier, (n_row - 1) + (n_col - 1) + (n_layer - 1))
 
     sends = []
@@ -197,13 +203,16 @@
         out_shape=jax.ShapeDtypeStruct((1,) + strip, jnp.bfloat16),
         in_specs=[
             pl.BlockSpec(memory_space=pl.ANY),
-            pl.BlockSpec(memory_space=pltpu.SMEM),
-            pl.BlockSpec(memory_space=pl.ANY),
-            pl.BlockSpec(memory_space=pltpu.SMEM),
-            pl.BlockSpec(memory_space=pltpu.SMEM),
+            pl.BlockSpec(memory_space=pl.ANY),
+            pl.BlockSpec(memory_space=pl.ANY),
+            pl.BlockSpec(memory_space=pl.ANY),
+            pl.BlockSpec(memory_space=pl.ANY),
         ],
         out_specs=pl.BlockSpec(memory_space=pltpu.VMEM),
         scratch_shapes=[
+            pltpu.SMEM(a_cols.shape, jnp.int32),
+            pltpu.SMEM(p_cols.shape, jnp.int32),
+            pltpu.SMEM(c_cols.shape, jnp.int32),
             pltpu.VMEM((sections, rl, side, width), jnp.bfloat16),
             pltpu.VMEM((n_row, sections, rp, side, p_width), jnp.bfloat16),
             pltpu.VMEM((n_row, codes, LANES), jnp.int32),
@@ -214,14 +223,14 @@
             pltpu.VMEM(strip, jnp.float32),
             pltpu.VMEM((n_layer - 1,) + strip, jnp.bfloat16),
             pltpu.VMEM((n_layer - 1,) + strip, jnp.bfloat16),
-            dma((2,)),
+            dma((5,)),
             dma((n_row - 1,)), dma((n_row - 1,)),
             dma((n_row - 1,)), dma((n_row - 1,)),
             dma((n_col - 1,)), dma((n_col - 1,)),
             dma((n_layer - 1,)), dma((n_layer - 1,)),
         ],
         compiler_params=pltpu.CompilerParams(
-            collective_id=0, has_side_effects=True, vmem_limit_bytes=40 * 2**20),
+            collective_id=0, has_side_effects=True, vmem_limit_bytes=63 * 2**20),
     )(a_blocks, a_cols, p_blocks, p_cols, c_cols)
 
 

time: 26.4 us -> 23.5 us (0.89)
  local copies, waits for them, and re-layouts: 4.53 us -> 1.47 us
  Pallas kernels: 21.6 us -> 21.9 us
    unnamed x11 -> x1, local copies, waits for them, and re-layouts: 4.53 us -> 1.47 us
where the time goes in v2:
time: 23.5 us; the launch traced here: 23.3 us
  Pallas kernels  21.9 us (93%)
  local copies, waits for them, and re-layouts  1.47 us (6%)
    pallas_call x1, Pallas kernels, local(): pl.pallas_call(functools.partial(kernel, dims), out_shape=jax.ShapeDtypeS...  21.9 us
    unnamed x1, local copies, waits for them, and re-layouts  1.47 us

profile of v2, /device:TPU:0, one launch (start us, length us, event | category | flops | bytes accessed | tf_op | source)
XLA Modules:
  0.0 23.3 jit_solution(2859789493694541140)
XLA Ops:
  0.0 21.9 %shard_map.55 = bf16[1,1,64,512]{3,2,1,0:T(8,128)(2,1)} custom-call(bf16[1,2,2,64,512]{4,3,2,1,0:T(8,128)(2,1)} %a_hbm.1, s32[1,2,2,8]{3,2,1,0:T(2,128)} %a_cols_hbm.1, bf16[1,2,1,2,64,256]{5,4,3,2,1,0:T(8,128)(2,1)} %p_hbm.1, s32[1,2,1,2,4]{4,3,2,1,0:T(2,128)} %p_cols_hbm.1, s32[1,4,8]{2,1,0:T(4,128)} %c_cols_hbm.1), custom_call_target="tpu_custom_call" | custom-call | tf_op jit(solution)/shard_map/pallas_call | solution.py:201
  21.9 1.5 %copy.7 = bf16[1,1,64,512]{3,2,1,0:T(8,128)(2,1)} copy(bf16[1,1,64,512]{3,2,1,0:T(8,128)(2,1)} %shard_map.55) | data formatting | bytes 131072

commit v3 on v2

v3 whole, which is shorter than its diff:
```python
import functools

import jax
import jax.numpy as jnp
from jax import lax
from jax.experimental import pallas as pl
from jax.experimental.pallas import tpu as pltpu
from jax.sharding import PartitionSpec as P

MESH = pl.DeviceIdType.MESH
LANES = 128
NCC = 16


def partner(me, d, n):
    out = 0
    bit = 1
    while bit < n:
        out = out + lax.rem(lax.div(me, bit) + ((d // bit) % 2), 2) * bit
        bit *= 2
    return out


def pair_codes(values, half):
    lane = lax.broadcasted_iota(jnp.int32, (1, LANES), 1)
    low = lane < half
    codes = []
    for p in range(len(values) // 2):
        codes.append(jnp.where(low, values[2 * p], values[2 * p + 1]))
        codes.append(jnp.where(low, values[2 * p + 1], values[2 * p]))
    return codes


def pair_tiles(x, half):
    tiles = []
    for p in range(x.shape[1] // LANES):
        tile = x[:, p * LANES:(p + 1) * LANES].astype(jnp.float32)
        tiles.append(tile)
        tiles.append(pltpu.roll(tile, half, axis=1))
    return tiles


def select4(lane, q, parts):
    out = parts[3]
    for g in (2, 1, 0):
        out = jnp.where(lane < (g + 1) * q, parts[g], out)
    return out


ORDER = (0, 2, 1, 3)


def pack(t0, t1, even, q):
    return jnp.where(even, t0, pltpu.roll(t1, q, axis=1)), jnp.where(even, pltpu.roll(t0, LANES - q, axis=1), t1)


def kernel(dims, a_hbm, a_cols_hbm, p_hbm, p_cols_hbm, c_cols_hbm, out_ref,
           a_cols, p_cols, c_cols, a_v, p_v, p_all, code_all, at_all, spread, t_acc, t_pick, own, c_send, c_recv,
           in_sem, ps, pr, cs, cr, as_, ar, zs, zr):
    n_row, n_col, n_layer = dims
    sections, rl, side, width = a_v.shape
    rp = p_all.shape[3]
    group = at_all.shape[0] * rl
    own_rows = c_send.shape[2]
    kc = c_cols.shape[2]
    quarter = side // 2
    tiles_t = NCC * quarter // LANES
    my_row, my_col, my_layer = (lax.axis_index(x) for x in ("row", "col", "layer"))

    barrier = pltpu.get_barrier_semaphore()
    for axis, me, n in (("row", my_row, n_row), ("col", my_col, n_col), ("layer", my_layer, n_layer)):
        for d in range(1, n):
            pl.semaphore_signal(barrier, inc=1, device_id={axis: partner(me, d, n)}, device_id_type=MESH)

    load_p = pltpu.make_async_copy(p_hbm.at[0, :, 0], p_v, in_sem.at[0])
    load_a = pltpu.make_async_copy(a_hbm.at[0], a_v, in_sem.at[1])
    load_pc = pltpu.make_async_copy(p_cols_hbm, p_cols, in_sem.at[2])
    load_ac = pltpu.make_async_copy(a_cols_hbm, a_cols, in_sem.at[3])
    load_cc = pltpu.make_async_copy(c_cols_hbm, c_cols, in_sem.at[4])
    for load in (load_p, load_pc, load_a, load_ac, load_cc):
        load.start()

    lane = lax.broadcasted_iota(jnp.int32, (side, LANES), 1)
    lane1 = lax.broadcasted_iota(jnp.int32, (1, LANES), 1)
    even = lax.rem(lax.div(lane, quarter), 2) == 0
    second = jnp.where(lane < side, 0, 1)
    fourth = lax.div(lane, quarter)

    load_pc.wait()
    for s in range(sections):
        for r in range(rp):
            cols = [p_cols[0, s, 0, r, j] for j in range(4)]
            for k in range(4):
                code = select4(lane1, quarter, [cols[ORDER[(g - k) % 4]] for g in range(4)])
                at = (s * rp + r) * 4 + k
                code_all[my_row, at:at + 1, :] = code
    load_p.wait()
    for s in range(sections):
        for r in range(rp):
            x = p_v[s, r].astype(jnp.float32)
            halves = pack(x[:, :LANES], x[:, LANES:], even, quarter)
            for h in range(2):
                p_all[h, my_row, s, r] = halves[h].astype(jnp.bfloat16)

    load_cc.wait()
    pl.semaphore_wait(barrier, (n_row - 1) + (n_col - 1) + (n_layer - 1))

    sends = []
    p_copies = [[], []]
    code_copies = []
    for d in range(1, n_row):
        to = {"row": partner(my_row, d, n_row)}
        code_copies.append(pltpu.make_async_remote_copy(
            code_all.at[my_row], code_all.at[my_row], cs.at[d - 1], cr.at[d - 1], device_id=to, device_id_type=MESH))
        for h in range(2):
            p_copies[h].append(pltpu.make_async_remote_copy(
                p_all.at[h, my_row], p_all.at[h, my_row], ps.at[h, d - 1], pr.at[h, d - 1],
                device_id=to, device_id_type=MESH))
    for copy in code_copies + p_copies[0]:
        copy.start()
    sends += code_copies

    load_ac.wait()
    load_a.wait()
    for s in range(sections):
        for i in range(rl):
            codes = pair_codes([a_cols[0, s, i, k] for k in range(width // side)], side)
            codes = [jnp.broadcast_to(code, (side, LANES)) for code in codes]
            tiles = pair_tiles(a_v[s, i], side)
            for q in range(n_row * rp // 2):
                total = jnp.zeros((side, LANES), jnp.float32)
                for code, tile in zip(codes, tiles):
                    total = total + jnp.where(code == 2 * q + second, tile, 0.0)
                slot = 2 * q // rp
                start = (s * rp + 2 * q % rp) * side
                at_all[my_col, slot, i * side:(i + 1) * side, start:start + LANES] = total.astype(jnp.bfloat16)
    a_copies = []
    for d in range(1, n_col):
        copy = pltpu.make_async_remote_copy(
            at_all.at[my_col], at_all.at[my_col], as_.at[d - 1], ar.at[d - 1],
            device_id={"col": partner(my_col, d, n_col)}, device_id_type=MESH)
        copy.start()
        a_copies.append(copy)
        sends.append(copy)

    def spread_rows(h, slot, to):
        for s in range(sections):
            for r in range(rp):
                tile = p_all[h, slot, s, r].astype(jnp.float32)
                tiles = [tile] + [pltpu.roll(tile, k * quarter, axis=1) for k in range(1, 4)]
                codes = []
                for k in range(4):
                    at = (s * rp + r) * 4 + k
                    codes.append(jnp.broadcast_to(code_all[slot, at:at + 1, :], (side, LANES)))
                for q in range(tiles_t):
                    total = jnp.zeros((side, LANES), jnp.float32)
                    for code, turned in zip(codes, tiles):
                        total = jnp.where(code == 4 * q + fourth, turned, total)
                    first = (s * rp + r) * side
                    spread[h, to, first:first + side, q * LANES:(q + 1) * LANES] = total.astype(jnp.bfloat16)

    step_cols = 2 * LANES

    def multiply(h, d):
        left = at_all[:, partner(my_row, d, n_row)].reshape(group * side, sections * rp * side)
        for n in range(0, NCC * quarter, step_cols):
            part = jnp.dot(left, spread[h, d, :, n:n + step_cols], preferred_element_type=jnp.float32)
            if d > 0:
                part = part + t_acc[h, :, n:n + step_cols]
            if d < n_row - 1:
                t_acc[h, :, n:n + step_cols] = part
                continue
            for i in range(group):
                for e in range(step_cols // LANES):
                    tile = part[i * side:(i + 1) * side, e * LANES:(e + 1) * LANES]
                    q = n // LANES + e
                    t_pick[h, i, q] = tile
                    for k in range(1, 4):
                        t_pick[h, i, k * tiles_t + q] = pltpu.roll(tile, k * quarter, axis=1)

    def pick(h, i, u):
        parts = []
        for g in range(4):
            c = c_cols[0, i, 4 * u + ORDER[g]]
            turn = lax.rem(g + 4 - lax.rem(c, 4), 4)
            parts.append(t_pick[h, i, turn * tiles_t + lax.div(c, 4)])
        return select4(lane, quarter, parts)

    for h in range(2):
        spread_rows(h, my_row, 0)
    for copy in p_copies[0]:
        copy.wait_send()
    for copy in p_copies[1]:
        copy.start()
    sends += p_copies[1]
    for copy in a_copies:
        copy.wait_recv()
    for h in range(2):
        multiply(h, 0)

    z_copies = [[], []]
    for h in range(2):
        for d in range(1, n_row):
            if h == 0:
                code_copies[d - 1].wait_recv()
            p_copies[h][d - 1].wait_recv()
            spread_rows(h, partner(my_row, d, n_row), d)
            multiply(h, d)
        for d in range(n_layer - 1, 0, -1):
            dst = partner(my_layer, d, n_layer)
            for o in range(own_rows):
                for u in range(kc // 4):
                    c_send[h, d - 1, o, :, u * LANES:(u + 1) * LANES] = pick(
                        h, dst * own_rows + o, u).astype(jnp.bfloat16)
            copy = pltpu.make_async_remote_copy(
                c_send.at[h, d - 1], c_recv.at[h, d - 1], zs.at[h, d - 1], zr.at[h, d - 1],
                device_id={"layer": dst}, device_id_type=MESH)
            copy.start()
            z_copies[h].append(copy)
            sends.append(copy)
        for o in range(own_rows):
            for u in range(kc // 4):
                own[h, o, :, u * LANES:(u + 1) * LANES] = pick(h, my_layer * own_rows + o, u)

    for h in range(2):
        for copy in z_copies[h]:
            copy.wait_recv()
        total = own[h]
        for d in range(1, n_layer):
            total = total + c_recv[h, d - 1].astype(jnp.float32)
        own[h] = total
    for o in range(own_rows):
        for u in range(kc // 4):
            h0 = own[0, o, :, u * LANES:(u + 1) * LANES]
            h1 = own[1, o, :, u * LANES:(u + 1) * LANES]
            for e, tile in enumerate(pack(h0, h1, even, quarter)):
                at = (2 * u + e) * LANES
                out_ref[0, o, :, at:at + LANES] = tile.astype(jnp.bfloat16)
    for copy in sends:
        copy.wait_send()


def local(dims, a_blocks, a_cols, p_blocks, p_cols, c_cols):
    n_row, n_col, n_layer = dims
    sections, rl, side, width = a_blocks.shape[1:]
    rp, p_width = p_blocks.shape[3], p_blocks.shape[5]
    group, kc = c_cols.shape[1:]
    own_rows = group // n_layer
    strip = (own_rows, side, kc * side)
    half_strip = (own_rows, side, kc * side // 2)
    depth = sections * rp * side
    dma = pltpu.SemaphoreType.DMA
    return pl.pallas_call(
        functools.partial(kernel, dims),
        out_shape=jax.ShapeDtypeStruct((1,) + strip, jnp.bfloat16),
        in_specs=[pl.BlockSpec(memory_space=pl.ANY)] * 5,
        out_specs=pl.BlockSpec(memory_space=pltpu.VMEM),
        scratch_shapes=[
            pltpu.SMEM(a_cols.shape, jnp.int32),
            pltpu.SMEM(p_cols.shape, jnp.int32),
            pltpu.SMEM(c_cols.shape, jnp.int32),
            pltpu.VMEM((sections, rl, side, width), jnp.bfloat16),
            pltpu.VMEM((sections, rp, side, p_width), jnp.bfloat16),
            pltpu.VMEM((2, n_row, sections, rp, side, LANES), jnp.bfloat16),
            pltpu.VMEM((n_row, sections * rp * 4, LANES), jnp.int32),
            pltpu.VMEM((n_col, n_row, rl * side, depth), jnp.bfloat16),
            pltpu.VMEM((2, n_row, depth, NCC * side // 2), jnp.bfloat16),
            pltpu.VMEM((2, group * side, NCC * side // 2), jnp.float32),
            pltpu.VMEM((2, group, NCC, side, LANES), jnp.float32),
            pltpu.VMEM((2,) + half_strip, jnp.float32),
            pltpu.VMEM((2, n_layer - 1) + half_strip, jnp.bfloat16),
            pltpu.VMEM((2, n_layer - 1) + half_strip, jnp.bfloat16),
            dma((5,)),
            dma((2, n_row - 1)), dma((2, n_row - 1)),
            dma((n_row - 1,)), dma((n_row - 1,)),
            dma((n_col - 1,)), dma((n_col - 1,)),
            dma((2, n_layer - 1)), dma((2, n_layer - 1)),
        ],
        compiler_params=pltpu.CompilerParams(
            collective_id=0, has_side_effects=True, vmem_limit_bytes=63 * 2**20),
    )(a_blocks, a_cols, p_blocks, p_cols, c_cols)


def solution(mesh):
    dims = tuple(mesh.shape[x] for x in ("row", "col", "layer"))
    return jax.shard_map(
        functools.partial(local, dims),
        mesh=mesh,
        in_specs=(
            P("layer", None, ("row", "col"), None, None),
            P("layer", None, ("row", "col"), None),
            P("layer", None, "col", "row", None, None),
            P("layer", None, "col", "row", None),
            P("col", "row", None),
        ),
        out_specs=P("col", ("row", "layer"), None, None),
        check_vma=False,
    )
```

time: 23.5 us -> 21.5 us (0.915)
  Pallas kernels: 21.9 us -> 19.9 us
    pallas_call x1, Pallas kernels: 21.9 us -> 19.9 us  [local(): pl.pallas_call(functools.partial(kernel, dims), out_shape=jax.ShapeDtypeS...]
where the time goes in v3:
time: 21.5 us; the launch traced here: 21.3 us
  Pallas kernels  19.9 us (93%)
  local copies, waits for them, and re-layouts  1.47 us (7%)
    pallas_call x1, Pallas kernels, local(): pl.pallas_call(functools.partial(kernel, dims), out_shape=jax.ShapeDtypeS...  19.9 us
    unnamed x1, local copies, waits for them, and re-layouts  1.47 us

profile of v3, /device:TPU:0, one launch (start us, length us, event | category | flops | bytes accessed | tf_op | source)
XLA Modules:
  0.0 21.3 jit_solution(8660012331754625916)
XLA Ops:
  0.0 19.9 %shard_map.55 = bf16[1,1,64,512]{3,2,1,0:T(8,128)(2,1)} custom-call(bf16[1,2,2,64,512]{4,3,2,1,0:T(8,128)(2,1)} %a_hbm.1, s32[1,2,2,8]{3,2,1,0:T(2,128)} %a_cols_hbm.1, bf16[1,2,1,2,64,256]{5,4,3,2,1,0:T(8,128)(2,1)} %p_hbm.1, s32[1,2,1,2,4]{4,3,2,1,0:T(2,128)} %p_cols_hbm.1, s32[1,4,8]{2,1,0:T(4,128)} %c_cols_hbm.1), custom_call_target="tpu_custom_call" | custom-call | tf_op jit(solution)/shard_map/pallas_call | solution.py:253
  19.9 1.5 %copy.7 = bf16[1,1,64,512]{3,2,1,0:T(8,128)(2,1)} copy(bf16[1,1,64,512]{3,2,1,0:T(8,128)(2,1)} %shard_map.55) | data formatting | bytes 131072
